TPU v7x, 512 devices: a whole 4x8x8 slice. The times are simulated.
512 devices in a mesh: dp: 32 (over x, y), seq: 16 (over z, core).
Axes of the slice: x: 4, y: 8, z: 8, core: 2. Of those that a mesh axis runs over, the one named last changes fastest.
Arguments:
- volume: bfloat16 [32, 3072, 1024], P('dp', 'seq')
- cotangent: bfloat16 [32, 3072, 1024], P('dp', 'seq'), may hold values from -6 to 6
- weights: bfloat16 [1024, 3, 1024], P('dp')
- pairs: int32 [32, 16, 24, 4], P('dp', 'seq'), may hold values from 0 to 23, as said below
- valid: int32 [32, 16, 24, 4], P('dp', 'seq'), may hold values from 0 to 1, as said below
Outputs:
- attended: bfloat16 [32, 3072, 1024], P('dp', 'seq')
- weight_grad: float32 [1024, 3, 1024], P('dp', None, 'seq')
Inputs may be any that keep to these rules, and one draw needn't show every extreme that they name: `pairs`: slot 0 of query block b holds b; the key blocks of one query block's slots are distinct. `valid`: slot 0 is always 1.
All inputs are finite; a program needn't handle non-finite values.
Results may differ from a plain program's by a relative error of at most 0.03.
Values may be sent and summed in bfloat16 or wider, within the bound.
No kernel may reach another device: no remote copies, remote signals or barrier semaphores. Data moves between devices by JAX's collectives and lax.ppermute only.
A program may use at most 64 MiB of HBM per device.

v0:
```python
import math
import jax
import jax.numpy as jnp
from jax import lax
from jax.sharding import PartitionSpec as P

HD = 64


def head_pass(queries, keys_all, values_all, upstream, pair_list, pair_live):
    block_count, slot_count = pair_list.shape
    all_rows, head_size = queries.shape
    block_rows = all_rows // block_count
    per_step = math.gcd(block_count, max(1, 512 // block_rows))
    steps_n = block_count // per_step
    scaling = head_size ** (-0.5)
    key_blocks = keys_all.reshape(block_count, block_rows, head_size)
    value_blocks = values_all.reshape(block_count, block_rows, head_size)
    block_index = jnp.arange(block_count, dtype=jnp.int32)

    def step(totals, sliced):
        key_total, value_total = totals
        query_rows, grad_rows, slot_blocks, slot_live = sliced
        key_rows = key_blocks[slot_blocks].reshape(per_step, slot_count * block_rows, head_size)
        value_rows = value_blocks[slot_blocks].reshape(per_step, slot_count * block_rows, head_size)
        live_cols = jnp.repeat(slot_live > 0, block_rows, axis=1)[:, None, :]
        scores = (
            jnp.einsum("nqd,nkd->nqk", query_rows, key_rows, preferred_element_type=jnp.float32)
            * scaling
        )
        row_max = jnp.max(jnp.where(live_cols, scores, -1e30), axis=-1, keepdims=True)
        exponent = jnp.where(live_cols, jnp.exp(scores - row_max), 0.0)
        prob_full = exponent / jnp.sum(exponent, axis=-1, keepdims=True)
        rounded = prob_full.astype(jnp.bfloat16)
        result = jnp.einsum(
            "nqk,nkd->nqd", rounded, value_rows, preferred_element_type=jnp.float32
        ).astype(jnp.bfloat16)
        value_grad = jnp.einsum(
            "nqk,nqd->nkd", rounded, grad_rows, preferred_element_type=jnp.float32
        )
        prob_grad = jnp.einsum(
            "nqd,nkd->nqk", grad_rows, value_rows, preferred_element_type=jnp.float32
        )
        row_dot = jnp.sum(
            grad_rows.astype(jnp.float32) * result.astype(jnp.float32), axis=-1, keepdims=True
        )
        score_grad = (prob_full * (prob_grad - row_dot) * scaling).astype(jnp.bfloat16)
        query_grad = jnp.einsum(
            "nqk,nkd->nqd", score_grad, key_rows, preferred_element_type=jnp.float32
        ).astype(jnp.bfloat16)
        key_grad = jnp.einsum(
            "nqk,nqd->nkd", score_grad, query_rows, preferred_element_type=jnp.float32
        )
        one_hot = (
            (slot_blocks.reshape(-1)[:, None] == block_index[None, :])
            & (slot_live.reshape(-1)[:, None] > 0)
        ).astype(jnp.float32)
        key_total = key_total + jnp.einsum(
            "jb,jrd->brd",
            one_hot,
            key_grad.reshape(per_step * slot_count, block_rows, head_size),
            precision=lax.Precision.HIGHEST,
        )
        value_total = value_total + jnp.einsum(
            "jb,jrd->brd",
            one_hot,
            value_grad.reshape(per_step * slot_count, block_rows, head_size),
            precision=lax.Precision.HIGHEST,
        )
        return ((key_total, value_total), (result, query_grad))

    empty_acc = jnp.zeros((block_count, block_rows, head_size), jnp.float32)
    sliced_all = (
        queries.reshape(steps_n, per_step, block_rows, head_size),
        upstream.reshape(steps_n, per_step, block_rows, head_size),
        pair_list.reshape(steps_n, per_step, slot_count),
        pair_live.reshape(steps_n, per_step, slot_count),
    )
    (key_total, value_total), (results, query_grads) = lax.scan(
        step, (empty_acc, empty_acc), sliced_all
    )
    return (
        results.reshape(all_rows, head_size),
        query_grads.reshape(all_rows, head_size),
        key_total.astype(jnp.bfloat16).reshape(all_rows, head_size),
        value_total.astype(jnp.bfloat16).reshape(all_rows, head_size),
    )


def local(volume, cotangent, weights, pairs, valid):
    seq_devices = lax.axis_size("seq")
    local_volume = volume[0]
    local_grad = cotangent[0]
    tok_count = local_volume.shape[0]
    width_all = local_grad.shape[1]
    local_cols = width_all // seq_devices
    all_rows = tok_count * seq_devices
    projected = jnp.einsum(
        "td,djc->tjc",
        local_volume,
        lax.all_gather(weights, "dp", axis=0, tiled=True),
        preferred_element_type=jnp.float32,
    )
    projected = projected.astype(jnp.bfloat16)
    head_inputs, head_grad = (
        lax.all_to_all(projected, "seq", split_axis=2, concat_axis=0, tiled=True),
        lax.all_to_all(
            local_grad.reshape(tok_count, 1, width_all),
            "seq",
            split_axis=2,
            concat_axis=0,
            tiled=True,
        ),
    )
    head_grad = head_grad.reshape(all_rows, local_cols)
    upper = HD
    result, query_grad, key_grad, value_grad = head_pass(
        head_inputs[:, 0, 0:upper],
        head_inputs[:, 1, 0:upper],
        head_inputs[:, 2, 0:upper],
        head_grad,
        pairs[0, 0],
        valid[0, 0],
    )
    grad_flat = jnp.stack([query_grad, key_grad, value_grad], axis=1).reshape(
        all_rows, 3 * local_cols
    )
    attended = lax.all_to_all(result, "seq", split_axis=0, concat_axis=1, tiled=True)
    local_sum = lax.dot_general(
        lax.all_gather(local_volume, "seq", axis=0, tiled=True),
        grad_flat,
        (((0,), (0,)), ((), ())),
        preferred_element_type=jnp.float32,
    )
    weight_part = (
        lax.psum_scatter(local_sum.astype(jnp.bfloat16), "dp", scatter_dimension=0, tiled=True)
        .astype(jnp.float32)
        .reshape(-1, 3, local_cols)
    )
    return (attended[None], weight_part)


def solution(mesh):
    return jax.shard_map(
        local,
        mesh=mesh,
        in_specs=(
            P("dp", "seq", None),
            P("dp", "seq", None),
            P("dp", None, None),
            P("dp", "seq", None, None),
            P("dp", "seq", None, None),
        ),
        out_specs=(P("dp", "seq", None), P("dp", None, "seq")),
        check_vma=False,
    )
```

profile of v0, /device:TPU:16, one launch (start us, length us, event | category | flops | bytes accessed | tf_op | source)
XLA Modules:
  0.0 509.1 jit_solution(6228003603930186872)
XLA Ops:
  8.7 2.4 copy.66
  11.6 4.1 reduce
  15.7 1.3 reshape.121
  17.1 10.4 %all-to-all-start.1 = ((bf16[16,2,6144]{2,1,0:T(2,128)(2,1)}), bf16[16,2,6144]{2,1,0:T(2,128)(2,1)S(1)}, u32[]{:S(2)}, u32[]{:S(2)}) async-start(bf16[16,2,6144]{2,1,0:T(2,128)(2,1)} %reshape.121), calls=%async_computation.1 | async-start | bytes 786432 | tf_op jit(solution)/shard_map/all_to_all | solution.py:107
  27.5 81.9 %all-gather.4.cloned.1.call-done = bf16[1024,3,1024]{2,0,1:T(8,128)(2,1)} async-done(((bf16[32,3,1024]{2,0,1:T(8,128)(2,1)}), bf16[1024,3,1024]{2,0,1:T(8,128)(2,1)}) %all-gather.4.cloned.1.call-update) | async-done | bytes 6291472 | tf_op jit(solution)/shard_map/all_gather | solution.py:101
  109.4 4.2 convolution_convert_fusion.2
  113.6 2.6 copy.63
  116.2 7.6 %all-to-all-start = ((bf16[192,3,1024]{0,1,2:T(4,128)(2,1)}), bf16[192,3,1024]{0,1,2:T(4,128)(2,1)S(1)}, u32[]{:S(2)}, u32[]{:S(2)}) async-start(bf16[192,3,1024]{0,1,2:T(4,128)(2,1)} %copy.63), calls=%async_computation | async-start | bytes 4194304 | tf_op jit(solution)/shard_map/all_to_all | solution.py:106
  125.4 2.0 reshape.122
  127.4 1.3 copy.95
  129.0 1.4 reshape_reshape.3
  130.4 57.3 %all-to-all-done = bf16[192,3,1024]{0,1,2:T(4,128)(2,1)S(1)} async-done(((bf16[192,3,1024]{0,1,2:T(4,128)(2,1)}), bf16[192,3,1024]{0,1,2:T(4,128)(2,1)S(1)}, u32[]{:S(2)}, u32[]{:S(2)}) %all-to-all-start) | async-done | bytes 1179680 | tf_op jit(solution)/shard_map/all_to_all | solution.py:106
  187.9 0.9 copy.65
  188.8 1.7 all_to_all.39
  190.6 1.2 copy.85
  191.7 1.2 copy.86
  192.9 1.1 reshape_squeeze.20
  194.0 83.2 %while.17 = (s32[]{:T(128)}, f32[24,128,64]{1,0,2:T(8,128)S(1)}, f32[24,128,64]{1,0,2:T(8,128)}, bf16[6,4,128,64]{2,1,0,3:T(4,128)(2,1)}, bf16[6,4,128,64]{2,1,0...) while((s32[]{:T(128)}, f32[24,128,64]{1,0,2:T(8,128)S(1)}, ...), condition=%wide.region_4.5_spmd.clone, body=%wide.region_0.4_spmd.clone.sunk | while | flops 280955456 | bytes 27224828 | solution.py:79
  194.7 1.8 gather_fusion.1
  196.6 0.9 constant_dynamic-slice_fusion.7
  198.9 1.8 gather_fusion
  200.7 0.9 constant_dynamic-slice_fusion.6
  207.0 0.9 copy-done.1
  208.7 1.8 gather_fusion.1
  210.4 0.9 constant_dynamic-slice_fusion.7
  212.8 1.8 gather_fusion
  214.6 0.9 constant_dynamic-slice_fusion.6
  220.8 0.9 copy-done.1
  222.5 1.8 gather_fusion.1
  226.7 1.8 gather_fusion
  234.7 0.9 copy-done.1
  236.4 1.8 gather_fusion.1
  240.5 1.8 gather_fusion
  248.6 0.9 copy-done.1
  250.2 1.8 gather_fusion.1
  252.0 0.9 constant_dynamic-slice_fusion.7
  254.4 1.8 gather_fusion
  256.2 0.9 constant_dynamic-slice_fusion.6
  262.4 0.9 copy-done.1
  264.1 1.8 gather_fusion.1
  268.2 1.8 gather_fusion
  276.3 0.9 copy-done.1
  277.4 0.9 copy-done.2
  279.0 4.2 fusion.34
  283.2 1.0 copy.87
  284.8 23.0 %all_to_all.49 = bf16[16,192,64]{1,2,0:T(8,128)(2,1)S(1)} all-to-all(bf16[16,192,64]{1,2,0:T(8,128)(2,1)S(1)} %copy.75), channel_id=1, replica_groups=mesh['dp'=32,'seq'=16] {'seq'}, dimensions={0} | all-to-all | bytes 786432 | tf_op jit(solution)/shard_map/all_to_all | solution.py:128
  307.8 0.9 copy.77
  308.7 191.4 %reduce-scatter.4.cloned.1.call-done = bf16[32,192]{1,0:T(8,128)(2,1)} async-done(((bf16[1024,192]{1,0:T(8,128)(2,1)}), bf16[32,192]{1,0:T(8,128)(2,1)}) %reduce-scatter.4.cloned.1.call-update) | async-done | bytes 12304
  (231 shorter events, 56.7 us)
Async XLA Ops:
  8.0 101.4 %all-gather.4.cloned.1.call-start = ((), (), s32[]{:S(2)}) async-start(), calls=%async_computation.4 | async-start | bytes 6488064 | tf_op jit(solution)/shard_map/all_gather | solution.py:101
  11.6 97.8 %copy-start.3 = (bf16[1,192,1024]{2,1,0:T(8,128)(2,1)S(1)}, bf16[1,192,1024]{2,1,0:T(8,128)(2,1)}, u32[]{:S(2)}) copy-start(bf16[1,192,1024]{2,1,0:T(8,128)(2,1)} %param.7) | copy-start | bytes 1179652
  17.1 99.1 %all-to-all-start.1 = ((bf16[16,2,6144]{2,1,0:T(2,128)(2,1)}), bf16[16,2,6144]{2,1,0:T(2,128)(2,1)S(1)}, u32[]{:S(2)}, u32[]{:S(2)}) async-start(bf16[16,2,6144]{2,1,0:T(2,128)(2,1)} %reshape.121), calls=%async_computation.1 | async-start | bytes 786432 | tf_op jit(solution)/shard_map/all_to_all | solution.py:107
  116.2 8.5 %copy-start.8 = (s32[1,1,24,4]{2,3,1,0:T(4,128)S(1)}, s32[1,1,24,4]{2,3,1,0:T(4,128)}, u32[]{:S(2)}) copy-start(s32[1,1,24,4]{2,3,1,0:T(4,128)} %param.10) | copy-start | bytes 1156
  116.2 9.2 %copy-start.9 = (s32[1,1,24,4]{2,3,1,0:T(4,128)S(1)}, s32[1,1,24,4]{2,3,1,0:T(4,128)}, u32[]{:S(2)}) copy-start(s32[1,1,24,4]{2,3,1,0:T(4,128)} %param.11) | copy-start | bytes 1156
  116.2 71.5 %all-to-all-start = ((bf16[192,3,1024]{0,1,2:T(4,128)(2,1)}), bf16[192,3,1024]{0,1,2:T(4,128)(2,1)S(1)}, u32[]{:S(2)}, u32[]{:S(2)}) async-start(bf16[192,3,1024]{0,1,2:T(4,128)(2,1)} %copy.63), calls=%async_computation | async-start | bytes 4194304 | tf_op jit(solution)/shard_map/all_to_all | solution.py:106
  123.8 155.2 %all-gather.6.cloned.1.call-start = ((), (), s32[]{:S(2)}) async-start(), calls=%async_computation.5 | async-start | bytes 6684672 | tf_op jit(solution)/shard_map/all_gather | solution.py:130
  124.4 375.7 %reduce-scatter.4.cloned.1.call-start = ((), (), s32[]{:S(2)}) async-start(), calls=%async_computation.6 | async-start | bytes 540672
  194.0 4.0 copy-start.6
  203.4 0.9 copy-start.7
  205.1 1.1 copy-start
  207.0 0.9 copy-start.1
  207.9 3.9 copy-start.6
  217.3 0.9 copy-start.7
  219.0 1.1 copy-start
  220.8 0.9 copy-start.1
  221.7 3.9 copy-start.6
  231.2 0.9 copy-start.7
  232.8 1.1 copy-start
  234.7 0.9 copy-start.1
  235.6 3.9 copy-start.6
  245.0 0.9 copy-start.7
  246.7 1.1 copy-start
  248.5 0.9 copy-start.1
  249.4 3.9 copy-start.6
  258.9 0.9 copy-start.7
  260.6 1.1 copy-start
  262.4 0.9 copy-start.1
  263.3 3.9 copy-start.6
  272.7 0.9 copy-start.7
  274.4 1.1 copy-start
  276.3 0.9 copy-start.1
  277.2 1.1 copy-start.2
  277.2 1.3 copy-start.5
  283.2 1.0 copy-start.4
Sparse Core Ops, SparseCore 0:
  12.0 97.3 all-gather.3
  284.4 215.6 reduce-scatter.3
Sparse Core Ops, SparseCore 1:
  126.4 77.8 all-gather.5
where the time goes:
time: 511 us; the launch traced here: 509 us
  waiting for transfers between devices  332 us (65%)
  local copies, waits for them, and re-layouts  76.9 us (15%)
  matrix products  27.8 us (5%)
  blocking collectives  23 us (5%)
  starting transfers between devices  18.3 us (4%)
  between operations  15.7 us (3%)
  other arithmetic  14.6 us (3%)
    unnamed x4, waiting for transfers between devices  193 us
    all_gather x1, waiting for transfers between devices, local(): lax.all_gather(weights, 'dp', axis=0, tiled=True)  81.9 us
    all_to_all x1, waiting for transfers between devices, local(): lax.all_to_all(projected, 'seq', split_axis=2, concat_axis=0, tiled=True)  57.3 us
    all_to_all x1, blocking collectives, local(): lax.all_to_all(result, 'seq', split_axis=0, concat_axis=1, tiled=True)  23 us
    unnamed x24, local copies, waits for them, and re-layouts  12.6 us
    gather x6, local copies, waits for them, and re-layouts, step(): key_blocks[slot_blocks]  10.7 us
    gather x6, local copies, waits for them, and re-layouts, step(): value_blocks[slot_blocks]  10.7 us
    dynamic_slice x12, local copies, waits for them, and re-layouts, head_pass(): lax.scan(step, (empty_acc, empty_acc), sliced_all)  10.5 us
  transfers between devices with their start and end apart: 5, of which 3 were waited for; matrix products, arithmetic and copies ran while one was open for 20% of the time, Pallas kernels for 0%

commit v1 on v0

--- a/solution.py
+++ b/solution.py
@@ -98,7 +98,9 @@
     projected = jnp.einsum(
         "td,djc->tjc",
         local_volume,
-        lax.all_gather(weights, "dp", axis=0, tiled=True),
+        jnp.concatenate(
+            lax.all_to_all(jnp.stack([weights] * lax.axis_size("dp")), "dp", 0, 0), axis=0
+        ),
         preferred_element_type=jnp.float32,
     )
     projected = projected.astype(jnp.bfloat16)

time: 511 us -> 580 us (1.14)
  waiting for transfers between devices: 332 us -> 397 us
  local copies, waits for them, and re-layouts: 76.9 us -> 83.3 us
    all_to_all x0 -> x1, waiting for transfers between devices: none -> 133 us  [local(): lax.all_to_all(jnp.stack([weights] * lax.axis_size('dp')), 'dp', 0, 0)]
    all_gather x1 -> x0, waiting for transfers between devices: 81.9 us -> none  [local(): lax.all_gather(weights, 'dp', axis=0, tiled=True)]
    unnamed x4 -> x3, waiting for transfers between devices: 193 us -> 205 us
    all_to_all x0 -> x1, starting transfers between devices: none -> 10.3 us  [local(): lax.all_to_all(jnp.stack([weights] * lax.axis_size('dp')), 'dp', 0, 0)]
    all_to_all x1, waiting for transfers between devices: 0.01 us -> 6.11 us  [local(): lax.all_to_all(local_grad.reshape(tok_count, 1, width_all), 'seq', split_...]
    unnamed x24 -> x26, local copies, waits for them, and re-layouts: 12.6 us -> 12.6 us
  transfers between devices with their start and end apart: 5 -> 5, of which waited for: 3 -> 4; matrix products, arithmetic and copies ran while one was open for 20% -> 18% of each run, Pallas kernels for 0% -> 0%
where the time goes in v1:
time: 580 us; the launch traced here: 578 us
  waiting for transfers between devices  397 us (68%)
  local copies, waits for them, and re-layouts  83.3 us (14%)
  matrix products  25.1 us (4%)
  blocking collectives  22.3 us (4%)
  starting transfers between devices  20.7 us (4%)
  other arithmetic  14.6 us (3%)
  between operations  14.3 us (2%)
    unnamed x3, waiting for transfers between devices  205 us
    all_to_all x1, waiting for transfers between devices, local(): lax.all_to_all(jnp.stack([weights] * lax.axis_size('dp')), 'dp', 0, 0)  133 us
    all_to_all x1, waiting for transfers between devices, local(): lax.all_to_all(projected, 'seq', split_axis=2, concat_axis=0, tiled=True)  52.7 us
    all_to_all x1, blocking collectives, local(): lax.all_to_all(result, 'seq', split_axis=0, concat_axis=1, tiled=True)  22.3 us
    unnamed x26, local copies, waits for them, and re-layouts  12.6 us
  transfers between devices with their start and end apart: 5, of which 4 were waited for; matrix products, arithmetic and copies ran while one was open for 18% of the time, Pallas kernels for 0%

profile of v1, /device:TPU:16, one launch (start us, length us, event | category | flops | bytes accessed | tf_op | source)
XLA Modules:
  0.0 578.0 jit_solution(10573282102306270525)
XLA Ops:
  7.2 4.4 stack.4
  11.5 10.3 %all-to-all-start = ((bf16[32,32,3,1024]{3,1,2,0:T(8,128)(2,1)}), bf16[32,32,3,1024]{3,1,2,0:T(8,128)(2,1)}, u32[]{:S(2)}, u32[]{:S(2)}) async-start(bf16[32,32,3,1024]{3,1,2,0:T(8,128)(2,1)} %stack.4), calls=%async_computation | async-start | bytes 12582912 | tf_op jit(solution)/shard_map/all_to_all | solution.py:102
  23.3 4.0 reduce
  27.3 1.3 reshape.127
  28.7 133.0 %all-to-all-done = bf16[32,32,3,1024]{3,1,2,0:T(8,128)(2,1)} async-done(((bf16[32,32,3,1024]{3,1,2,0:T(8,128)(2,1)}), bf16[32,32,3,1024]{3,1,2,0:T(8,128)(2,1)}, u32[]{:S(2)}, u32[]{:S(2)}) %all-to-all-start) | async-done | bytes 6291488 | tf_op jit(solution)/shard_map/all_to_all | solution.py:102
  161.6 6.4 %all-to-all-start.2 = ((bf16[16,2,6144]{2,1,0:T(2,128)(2,1)}), bf16[16,2,6144]{2,1,0:T(2,128)(2,1)S(1)}, u32[]{:S(2)}, u32[]{:S(2)}) async-start(bf16[16,2,6144]{2,1,0:T(2,128)(2,1)} %reshape.127), calls=%async_computation.2 | async-start | bytes 786432 | tf_op jit(solution)/shard_map/all_to_all | solution.py:109
  168.0 3.5 copy.64
  171.6 1.4 convolution_convert_fusion.2
  173.0 2.6 copy.65
  175.6 6.1 %all-to-all-done.2 = bf16[16,2,6144]{2,1,0:T(2,128)(2,1)S(1)} async-done(((bf16[16,2,6144]{2,1,0:T(2,128)(2,1)}), bf16[16,2,6144]{2,1,0:T(2,128)(2,1)S(1)}, u32[]{:S(2)}, u32[]{:S(2)}) %all-to-all-start.2) | async-done | bytes 393248 | tf_op jit(solution)/shard_map/all_to_all | solution.py:109
  181.7 3.7 all-to-all-start.1
  187.2 2.0 reshape.128
  189.2 1.3 copy.97
  190.8 1.4 reshape_reshape.3
  192.2 52.7 %all-to-all-done.1 = bf16[192,3,1024]{0,1,2:T(4,128)(2,1)S(1)} async-done(((bf16[192,3,1024]{0,1,2:T(4,128)(2,1)}), bf16[192,3,1024]{0,1,2:T(4,128)(2,1)S(1)}, u32[]{:S(2)}, u32[]{:S(2)}) %all-to-all-start.1) | async-done | bytes 1179680 | tf_op jit(solution)/shard_map/all_to_all | solution.py:108
  245.1 0.9 copy.67
  246.0 1.7 all_to_all.43
  247.8 1.2 copy.88
  249.0 1.2 copy.87
  250.2 1.1 reshape_squeeze.20
  251.2 83.2 %while.17 = (s32[]{:T(128)}, f32[24,128,64]{1,0,2:T(8,128)S(1)}, f32[24,128,64]{1,0,2:T(8,128)}, bf16[6,4,128,64]{2,1,0,3:T(4,128)(2,1)}, bf16[6,4,128,64]{2,1,0...) while((s32[]{:T(128)}, f32[24,128,64]{1,0,2:T(8,128)S(1)}, ...), condition=%wide.region_4.5_spmd.clone, body=%wide.region_0.4_spmd.clone.sunk | while | flops 280955456 | bytes 27224828 | solution.py:79
  252.0 1.8 gather_fusion.1
  253.9 0.9 constant_dynamic-slice_fusion.7
  256.2 1.8 gather_fusion
  258.0 0.9 constant_dynamic-slice_fusion.6
  264.3 0.9 copy-done.1
  265.9 1.8 gather_fusion.1
  267.7 0.9 constant_dynamic-slice_fusion.7
  270.1 1.8 gather_fusion
  278.1 0.9 copy-done.1
  279.8 1.8 gather_fusion.1
  283.9 1.8 gather_fusion
  292.0 0.9 copy-done.1
  293.7 1.8 gather_fusion.1
  297.8 1.8 gather_fusion
  305.8 0.9 copy-done.1
  307.5 1.8 gather_fusion.1
  311.7 1.8 gather_fusion
  319.7 0.9 copy-done.1
  321.4 1.8 gather_fusion.1
  325.5 1.8 gather_fusion
  333.6 0.9 copy-done.1
  334.7 0.9 copy-done.2
  336.3 4.2 fusion.34
  340.5 1.0 copy.89
  342.1 22.3 %all_to_all.54 = bf16[16,192,64]{1,2,0:T(8,128)(2,1)S(1)} all-to-all(bf16[16,192,64]{1,2,0:T(8,128)(2,1)S(1)} %copy.77), channel_id=1, replica_groups=mesh['dp'=32,'seq'=16] {'seq'}, dimensions={0} | all-to-all | bytes 786432 | tf_op jit(solution)/shard_map/all_to_all | solution.py:130
  364.4 0.9 copy.79
  365.3 204.4 %reduce-scatter.4.cloned.1.call-done = bf16[32,192]{1,0:T(8,128)(2,1)} async-done(((bf16[1024,192]{1,0:T(8,128)(2,1)}), bf16[32,192]{1,0:T(8,128)(2,1)}) %reduce-scatter.4.cloned.1.call-update) | async-done | bytes 12304
  (234 shorter events, 59.6 us)
Async XLA Ops:
  11.5 10.4 %copy-start.6 = (bf16[1,192,1024]{2,1,0:T(8,128)(2,1)S(1)}, bf16[1,192,1024]{2,1,0:T(8,128)(2,1)}, u32[]{:S(2)}) copy-start(bf16[1,192,1024]{2,1,0:T(8,128)(2,1)} %param.8) | copy-start | bytes 1179652
  11.5 150.1 %all-to-all-start = ((bf16[32,32,3,1024]{3,1,2,0:T(8,128)(2,1)}), bf16[32,32,3,1024]{3,1,2,0:T(8,128)(2,1)}, u32[]{:S(2)}, u32[]{:S(2)}) async-start(bf16[32,32,3,1024]{3,1,2,0:T(8,128)(2,1)} %stack.4), calls=%async_computation | async-start | bytes 12582912 | tf_op jit(solution)/shard_map/all_to_all | solution.py:102
  161.6 20.1 %all-to-all-start.2 = ((bf16[16,2,6144]{2,1,0:T(2,128)(2,1)}), bf16[16,2,6144]{2,1,0:T(2,128)(2,1)S(1)}, u32[]{:S(2)}, u32[]{:S(2)}) async-start(bf16[16,2,6144]{2,1,0:T(2,128)(2,1)} %reshape.127), calls=%async_computation.2 | async-start | bytes 786432 | tf_op jit(solution)/shard_map/all_to_all | solution.py:109
  168.0 3.6 copy-start.3
  175.6 10.9 %copy-start.9 = (s32[1,1,24,4]{2,3,1,0:T(4,128)S(1)}, s32[1,1,24,4]{2,3,1,0:T(4,128)}, u32[]{:S(2)}) copy-start(s32[1,1,24,4]{2,3,1,0:T(4,128)} %param.10) | copy-start | bytes 1156
  175.6 11.6 %copy-start.10 = (s32[1,1,24,4]{2,3,1,0:T(4,128)S(1)}, s32[1,1,24,4]{2,3,1,0:T(4,128)}, u32[]{:S(2)}) copy-start(s32[1,1,24,4]{2,3,1,0:T(4,128)} %param.11) | copy-start | bytes 1156
  181.7 63.2 %all-to-all-start.1 = ((bf16[192,3,1024]{0,1,2:T(4,128)(2,1)}), bf16[192,3,1024]{0,1,2:T(4,128)(2,1)S(1)}, u32[]{:S(2)}, u32[]{:S(2)}) async-start(bf16[192,3,1024]{0,1,2:T(4,128)(2,1)} %copy.65), calls=%async_computation.1 | async-start | bytes 4194304 | tf_op jit(solution)/shard_map/all_to_all | solution.py:108
  185.4 150.9 %all-gather.3.cloned.1.call-start = ((), (), s32[]{:S(2)}) async-start(), calls=%async_computation.5 | async-start | bytes 6684672 | tf_op jit(solution)/shard_map/all_gather | solution.py:132
  186.2 383.5 %reduce-scatter.4.cloned.1.call-start = ((), (), s32[]{:S(2)}) async-start(), calls=%async_computation.6 | async-start | bytes 540672
  251.2 4.0 copy-start.7
  260.7 0.9 copy-start.8
  262.4 1.1 copy-start
  264.2 0.9 copy-start.1
  265.1 3.9 copy-start.7
  274.6 0.9 copy-start.8
  276.3 1.1 copy-start
  278.1 0.9 copy-start.1
  279.0 3.9 copy-start.7
  288.4 0.9 copy-start.8
  290.1 1.1 copy-start
  292.0 0.9 copy-start.1
  292.9 3.9 copy-start.7
  302.3 0.9 copy-start.8
  304.0 1.1 copy-start
  305.8 0.9 copy-start.1
  306.7 3.9 copy-start.7
  316.2 0.9 copy-start.8
  317.8 1.1 copy-start
  319.7 0.9 copy-start.1
  320.6 3.9 copy-start.7
  330.0 0.9 copy-start.8
  331.7 1.1 copy-start
  333.6 0.9 copy-start.1
  334.5 1.1 copy-start.2
  334.5 1.3 copy-start.5
  340.5 1.0 copy-start.4
Sparse Core Ops, SparseCore 0:
  188.4 77.4 all-gather.2
  341.6 227.9 reduce-scatter.3
